TPU v7x, 512 devices: a whole 4x4x16 slice. The times are simulated.
512 devices in a mesh: dp: 32 (over z, core), tensor: 16 (over x, y).
Axes of the slice: x: 4, y: 4, z: 16, core: 2. Of those that a mesh axis runs over, the one named last changes fastest.
Arguments:
- gradient: bfloat16 [32, 3072, 4096], P('dp', None, 'tensor'), may hold values from -66 to 66, as said below
- error_in: bfloat16 [32, 3072, 4096], P('dp', None, 'tensor'), may hold values from -3 to 3
- q_start: float32 [16, 4096], P(None, 'tensor'), may hold values from -6 to 6
Outputs:
- error_out: bfloat16 [32, 3072, 4096], P('dp', None, 'tensor')
- q_factor: float32 [16, 4096], P(None, 'tensor')
Inputs may be any that keep to these rules, and one draw needn't show every extreme that they name: Each replica's gradient has independent entries with row and column scales.
All inputs are finite; a program needn't handle non-finite values.
Results may differ from a plain program's by a relative error of at most 0.001.
Values sent between devices are 32-bit elements; how exact they have to be, the bound alone decides.
A program may use at most 64 MiB of HBM per device.

v0:
```python
import jax
import jax.numpy as jnp
from jax import lax
from jax.sharding import PartitionSpec as P

ITERS = 2


def orthonormal(left_rows, gram):
    lower = jnp.linalg.cholesky(gram)
    return lax.linalg.triangular_solve(lower, left_rows, left_side=True, lower=True)


def per_device(gradient, error_in, q_start):
    replicas = lax.axis_size("dp")
    accumulated = gradient[0].astype(jnp.float32) + error_in[0].astype(jnp.float32)
    right = q_start
    left_orth = None
    for sweep in range(ITERS):
        left_term = lax.dot_general(
            right, accumulated, (((1,), (1,)), ((), ())), precision=lax.Precision.HIGHEST
        )
        left_share = lax.psum_scatter(left_term, "tensor", scatter_dimension=1, tiled=True)
        left_share = lax.psum(left_share, "dp") / replicas
        gram_part = jnp.dot(left_share, left_share.T, precision=lax.Precision.HIGHEST)
        gram = lax.psum(gram_part, "tensor")
        orth_share = orthonormal(left_share, gram)
        left_orth = lax.all_gather(orth_share, "tensor", axis=1, tiled=True)
        right_term = jnp.dot(left_orth, accumulated, precision=lax.Precision.HIGHEST)
        right = lax.psum(right_term, "dp") / replicas
    approx = jnp.dot(left_orth.T, right, precision=lax.Precision.HIGHEST)
    error_out = (accumulated - approx).astype(jnp.bfloat16)[None]
    return (error_out, right)


def solution(mesh):
    placed = (P("dp", None, "tensor"), P("dp", None, "tensor"), P(None, "tensor"))
    return jax.shard_map(
        per_device,
        mesh=mesh,
        in_specs=placed,
        out_specs=(P("dp", None, "tensor"), P(None, "tensor")),
        check_vma=False,
    )
```

profile of v0, /device:TPU:1, one launch (start us, length us, event | category | flops | bytes accessed | tf_op | source)
XLA Modules:
  0.0 708.1 jit_solution(8425251318781531973)
XLA Ops:
  7.2 0.0 copy-start
  7.2 0.0 reduce-scatter.7.cloned.1.call-start
  7.2 0.7 copy-done
  7.9 4.9 convolution_bitcast_fusion.1
  12.8 0.0 copy-start.2
  12.8 1.6 copy.23
  14.4 0.0 copy-start.1
  14.4 0.0 reduce-scatter.7.cloned.1.call-update
  14.4 0.0 reduce-scatter.9.cloned.1.call-start
  14.5 92.7 %reduce-scatter.7.cloned.1.call-done = f32[192,16]{1,0:T(8,128)} async-done(((f32[3072,16]{1,0:T(8,128)}), f32[192,16]{1,0:T(8,128)}) %reduce-scatter.7.cloned.1.call-update) | async-done | bytes 12304
  107.2 0.9 copy.24
  108.2 90.6 %psum.42 = f32[16,192]{1,0:T(8,128)S(1)} all-reduce(f32[16,192]{1,0:T(8,128)S(1)} %copy.24), channel_id=1, replica_groups=mesh['dp'=32,'tensor'=16] {'dp'}, use_global_device_ids=true, to_apply=%region_1.0 | all-reduce | flops 3072 | bytes 24576 | tf_op jit(solution)/shard_map/psum | solution.py:24
  198.8 0.1 fusion.13
  198.9 31.4 %psum.43 = f32[16,16]{0,1:T(8,128)S(1)} all-reduce(f32[16,16]{0,1:T(8,128)S(1)} %fusion.13), channel_id=1, replica_groups=mesh['dp'=32,'tensor'=16] {'tensor'}, use_global_device_ids=true, to_apply=%region_2.0 | all-reduce | flops 256 | bytes 2048 | tf_op jit(solution)/shard_map/psum | solution.py:26
  230.3 0.1 copy.16
  230.4 1.5 cholesky.44
  231.9 0.6 compare_reduce_fusion.1
  232.5 0.6 fusion.15
  233.2 1.2 custom-call.6
  234.4 0.2 convolution_bitcast_fusion.3
  234.6 15.5 %all-gather = f32[16,192,16]{1,2,0:T(8,128)S(1)} all-gather(f32[1,192,16]{1,2,0:T(8,128)S(1)} %convolution_bitcast_fusion.3), channel_id=1, replica_groups=mesh['dp'=32,'tensor'=16] {'tensor'}, dimensions={0}, use_global_device_ids=true | all-gather | bytes 208896 | tf_op jit(solution)/shard_map/all_gather | solution.py:28
  250.1 0.2 copy.17
  250.3 0.8 reshape.21
  251.1 0.0 copy-done.2
  251.1 0.0 copy-done.1
  251.1 2.5 fusion.5
  253.6 102.4 %psum.44 = f32[16,256]{1,0:T(8,128)S(1)} all-reduce(f32[16,256]{1,0:T(8,128)S(1)} %fusion.5), channel_id=1, replica_groups=mesh['dp'=32,'tensor'=16] {'dp'}, use_global_device_ids=true, to_apply=%region_5.8 | all-reduce | flops 4096 | bytes 32768 | tf_op jit(solution)/shard_map/psum | solution.py:30
  356.0 3.7 convolution_bitcast_fusion
  359.8 0.0 reduce-scatter.9.cloned.1.call-update
  359.8 88.6 %reduce-scatter.9.cloned.1.call-done = f32[192,16]{1,0:T(8,128)} async-done(((f32[3072,16]{1,0:T(8,128)}), f32[192,16]{1,0:T(8,128)}) %reduce-scatter.9.cloned.1.call-update) | async-done | bytes 12304
  448.4 0.9 copy.26
  449.4 90.6 %psum.45 = f32[16,192]{1,0:T(8,128)S(1)} all-reduce(f32[16,192]{1,0:T(8,128)S(1)} %copy.26), channel_id=1, replica_groups=mesh['dp'=32,'tensor'=16] {'dp'}, use_global_device_ids=true, to_apply=%region_7.10 | all-reduce | flops 3072 | bytes 24576 | tf_op jit(solution)/shard_map/psum | solution.py:24
  539.9 0.1 fusion.10
  540.1 31.4 %psum.46 = f32[16,16]{0,1:T(8,128)S(1)} all-reduce(f32[16,16]{0,1:T(8,128)S(1)} %fusion.10), channel_id=1, replica_groups=mesh['dp'=32,'tensor'=16] {'tensor'}, use_global_device_ids=true, to_apply=%region_8.11 | all-reduce | flops 256 | bytes 2048 | tf_op jit(solution)/shard_map/psum | solution.py:26
  571.5 0.1 copy.19
  571.6 1.5 cholesky.55
  573.1 0.6 compare_reduce_fusion
  573.7 0.6 fusion.16
  574.4 1.2 custom-call.7
  575.6 0.2 convolution_bitcast_fusion.2
  575.8 15.7 %all-gather.1 = f32[16,192,16]{1,2,0:T(8,128)S(1)} all-gather(f32[1,192,16]{1,2,0:T(8,128)S(1)} %convolution_bitcast_fusion.2), channel_id=1, replica_groups=mesh['dp'=32,'tensor'=16] {'tensor'}, dimensions={0}, use_global_device_ids=true | all-gather | bytes 208896 | tf_op jit(solution)/shard_map/all_gather | solution.py:28
  591.5 0.9 copy.20
  592.4 1.1 reshape.23
  593.4 1.6 fusion.2
  595.0 102.4 %psum.47 = f32[16,256]{1,0:T(8,128)S(1)} all-reduce(f32[16,256]{1,0:T(8,128)S(1)} %fusion.2), channel_id=1, replica_groups=mesh['dp'=32,'tensor'=16] {'dp'}, use_global_device_ids=true, to_apply=%region_9.12 | all-reduce | flops 4096 | bytes 32768 | tf_op jit(solution)/shard_map/psum | solution.py:30
  697.4 0.0 copy-start.3
  697.4 3.8 fusion.1
  701.3 0.0 copy-done.3
  (5 shorter events, 0.1 us)
Async XLA Ops:
  7.2 0.7 copy-start
  7.2 100.0 %reduce-scatter.7.cloned.1.call-start = ((), (), s32[]{:S(2)}) async-start(), calls=%async_computation.2 | async-start | bytes 1671168
  12.8 238.3 %copy-start.2 = (bf16[1,3072,256]{2,1,0:T(8,128)(2,1)S(1)}, bf16[1,3072,256]{2,1,0:T(8,128)(2,1)}, u32[]{:S(2)}) copy-start(bf16[1,3072,256]{2,1,0:T(8,128)(2,1)} %param.6) | copy-start | bytes 4718596
  14.4 236.7 %copy-start.1 = (bf16[1,3072,256]{2,1,0:T(8,128)(2,1)S(1)}, bf16[1,3072,256]{2,1,0:T(8,128)(2,1)}, u32[]{:S(2)}) copy-start(bf16[1,3072,256]{2,1,0:T(8,128)(2,1)} %param.7) | copy-start | bytes 4718596
  14.4 434.0 %reduce-scatter.9.cloned.1.call-start = ((), (), s32[]{:S(2)}) async-start(), calls=%async_computation.3 | async-start | bytes 1671168
  697.4 3.8 copy-start.3
Sparse Core Ops, SparseCore 0:
  14.5 92.6 reduce-scatter.6
  359.9 88.4 reduce-scatter.8
where the time goes:
time: 711 us; the launch traced here: 708 us
  blocking collectives  480 us (68%)
  waiting for transfers between devices  181 us (25%)
  matrix products  17.2 us (2%)
  between operations  14.1 us (2%)
  other arithmetic  8.03 us (1%)
  local copies, waits for them, and re-layouts  7.24 us (1%)
    psum x2, blocking collectives, per_device(): right = lax.psum(right_term, 'dp') / replicas  205 us
    unnamed x4, waiting for transfers between devices  181 us
    psum x2, blocking collectives, per_device(): left_share = lax.psum(left_share, 'dp') / replicas  181 us
    psum x2, blocking collectives, per_device(): gram = lax.psum(gram_part, 'tensor')  62.9 us
    all_gather x2, blocking collectives, per_device(): left_orth = lax.all_gather(orth_share, 'tensor', axis=1, tiled=True)  31.2 us
  transfers between devices with their start and end apart: 2, of which 2 were waited for; matrix products, arithmetic and copies ran while one was open for 0% of the time, Pallas kernels for 0%

commit v1 on v0

v1 whole, which is shorter than its diff:
```python
import jax
import jax.numpy as jnp
from jax import lax
from jax.experimental import pallas as pl
from jax.experimental.pallas import tpu as pltpu
from jax.sharding import PartitionSpec as P

MESH = pl.DeviceIdType.MESH
F32 = jnp.float32
HIGH = lax.Precision.HIGHEST

RANK = 16
LANES = 128
NZ = 16
NT = 16
CHUNKS = 2


def dot_nn(a, b):
    return lax.dot_general(a, b, (((1,), (0,)), ((), ())), precision=HIGH, preferred_element_type=F32)


def dot_nt(a, b):
    return lax.dot_general(a, b, (((1,), (1,)), ((), ())), precision=HIGH, preferred_element_type=F32)


def inverse_factor(gram):
    rows = lax.broadcasted_iota(jnp.int32, (RANK, LANES), 0)
    lanes = lax.broadcasted_iota(jnp.int32, (RANK, LANES), 1)
    both = gram + (lanes == rows + RANK).astype(F32)
    for j in range(RANK):
        column = both[:, j : j + 1]
        scale = 1.0 / jnp.sqrt(column[j : j + 1, :])
        pivot = both[j : j + 1, :] * scale
        step = both - (column * scale) * pivot
        both = jnp.where(rows == j, pivot, jnp.where(rows > j, step, both))
    return both[:, RANK : 2 * RANK]


def compress(
    g_hbm, e_hbm, q_ref, orth_ref, right_ref,
    g_ref, e_ref, own, cross, cross_in, ring, mean, share, shares, term, pair, near, far, halves, gathered,
    load_sem, cross_send, cross_recv, ring_send, ring_recv, share_send, share_recv,
    pair_send, pair_recv, near_send, near_recv, far_send, far_recv, half_send, half_recv,
    gather_send, gather_recv, pass_send, pass_recv,
):
    dp, tensor = lax.axis_index("dp"), lax.axis_index("tensor")
    z, core = dp // 2, dp % 2
    block = own.shape[1]
    other = 1 - core

    loads = [
        pltpu.make_async_copy(g_hbm.at[0], g_ref, load_sem.at[0]),
        pltpu.make_async_copy(e_hbm.at[0], e_ref, load_sem.at[1]),
    ]
    for load in loads:
        load.start()

    sibling = (z * 2 + other, tensor)

    def along_z(hops):
        return (lax.rem(z + hops + NZ, NZ) * 2 + core, tensor)

    def in_plane(k):
        return (dp, lax.rem(tensor + k, NT))

    barrier = pltpu.get_barrier_semaphore()
    pl.semaphore_signal(barrier, inc=1, device_id=sibling, device_id_type=MESH)
    for k in range(1, NZ):
        pl.semaphore_signal(barrier, inc=1, device_id=along_z(k), device_id_type=MESH)
    for k in range(1, NT):
        pl.semaphore_signal(barrier, inc=1, device_id=in_plane(k), device_id_type=MESH)
    mean[...] = jnp.zeros_like(mean)
    for load in loads:
        load.wait()
    pl.semaphore_wait(barrier, NZ + NT - 1)

    def send(src, dst, send_sem, recv_sem, device):
        copy = pltpu.make_async_remote_copy(
            src_ref=src, dst_ref=dst, send_sem=send_sem, recv_sem=recv_sem, device_id=device, device_id_type=MESH
        )
        copy.start()
        return copy

    sent = []

    def accumulated(index):
        rows = pl.ds(pl.multiple_of(index * block, block), block)
        return g_ref[rows, :].astype(F32) + e_ref[rows, :].astype(F32)

    up = [lax.rem(z + 8 - k, NZ) for k in range(8)]
    down = [lax.rem(z + 9 + k, NZ) for k in range(7)]
    order = []
    for k in range(8):
        order.append(up[k])
        if k < 7:
            order.append(down[k])
    order.append(z)
    crossing = []
    for i, j in enumerate(order):
        cross[i] = accumulated(2 * j + other)
        crossing.append(send(cross.at[i], cross_in.at[i], cross_send.at[i], cross_recv.at[i], sibling))
    sent += crossing

    part = block // CHUNKS

    def ring_step(direction, k, target):
        copies = []
        for c in range(CHUNKS):
            rows = pl.ds(c * part, part)
            copies.append(
                send(
                    own.at[target, rows], ring.at[direction, k, rows],
                    ring_send.at[direction, k, c], ring_recv.at[direction, k, c],
                    along_z(1 if direction == 0 else -1),
                )
            )
        return copies

    ring_up, ring_down = [], []
    for i, j in enumerate(order):
        mine = accumulated(2 * j + core)
        crossing[i].wait_recv()
        own[j] = mine + cross_in[i]
        if i == 0:
            ring_up = ring_step(0, 0, j)
        if i == 1:
            ring_down = ring_step(1, 0, j)

    def take(copies, direction, k, target, onward):
        nexts = []
        for c in range(CHUNKS):
            rows = pl.ds(c * part, part)
            copies[c].wait_recv()
            own[target, rows, :] = own[target, rows, :] + ring[direction, k, rows, :]
            if onward:
                nexts.append(
                    send(
                        own.at[target, rows], ring.at[direction, k + 1, rows],
                        ring_send.at[direction, k + 1, c], ring_recv.at[direction, k + 1, c],
                        along_z(1 if direction == 0 else -1),
                    )
                )
        return nexts

    for k in range(1, 9):
        sent += ring_up
        if k < 8:
            ring_up = take(ring_up, 0, k - 1, up[k], True)
        if k < 8:
            sent += ring_down
            if k < 7:
                ring_down = take(ring_down, 1, k - 1, down[k], True)
            else:
                take(ring_down, 1, k - 1, z, False)
        if k == 8:
            take(ring_up, 0, k - 1, z, False)
    mean[0:block, :] = own[z] * (1.0 / 32.0)

    def sum_in_plane(sweep, value):
        share[sweep] = value
        copies = []
        for k in range(1, NT):
            copies.append(
                send(
                    share.at[sweep], shares.at[sweep, tensor],
                    share_send.at[sweep, k], share_recv.at[sweep, k], in_plane(k),
                )
            )
        shares[sweep, tensor] = value
        return copies

    def plane_total(sweep, copies):
        for copy in copies:
            copy.wait_recv()
        total = shares[sweep, 0]
        for k in range(1, NT):
            total = total + shares[sweep, k]
        return total

    def sum_along_z(sweep, value):
        half = term.shape[1] // 2
        term[sweep] = value
        group, place = z // 4, z % 4
        swap = send(
            term.at[sweep, pl.ds(other * half, half)], pair.at[sweep], pair_send.at[sweep], pair_recv.at[sweep], sibling
        )
        sent.append(swap)
        swap.wait_recv()
        near[sweep, place] = term[sweep, pl.ds(core * half, half), :] + pair[sweep]
        copies = []
        for k in range(1, 4):
            device = ((group * 4 + (place + k) % 4) * 2 + core, tensor)
            copies.append(
                send(
                    near.at[sweep, place], near.at[sweep, place],
                    near_send.at[sweep, k], near_recv.at[sweep, k], device,
                )
            )
        for copy in copies:
            copy.wait_recv()
        sent.extend(copies)
        far[sweep, group] = near[sweep, 0] + near[sweep, 1] + near[sweep, 2] + near[sweep, 3]
        copies = []
        for k in (2, 1, 3):
            copies.append(
                send(
                    far.at[sweep, group], far.at[sweep, group],
                    far_send.at[sweep, k], far_recv.at[sweep, k], along_z(4 * k),
                )
            )
        return copies

    def z_total(sweep, copies):
        for copy in copies:
            copy.wait_recv()
        sent.extend(copies)
        halves[sweep, core] = far[sweep, 0] + far[sweep, 1] + far[sweep, 2] + far[sweep, 3]
        swap = send(
            halves.at[sweep, core], halves.at[sweep, core], half_send.at[sweep], half_recv.at[sweep], sibling
        )
        swap.wait_recv()
        sent.append(swap)

    def z_term(left):
        wide = dot_nn(left, mean[...])
        gram = jnp.concatenate([dot_nt(left, left), jnp.zeros((RANK, LANES - RANK), F32)], axis=1)
        return jnp.concatenate([wide[:, :LANES], gram[:8], wide[:, LANES:], gram[8:]], axis=0)

    copies = sum_in_plane(0, dot_nt(q_ref[...], mean[...]))
    left = plane_total(0, copies)
    sent += copies
    z_total(0, sum_along_z(0, z_term(left)))
    right = jnp.concatenate([halves[0, 0, 0:RANK, :], halves[0, 1, 0:RANK, :]], axis=1)
    copies = sum_in_plane(1, dot_nt(right, mean[...]))
    gram = jnp.concatenate([halves[0, 0, RANK:, :], halves[0, 1, RANK:, :]], axis=0)
    inverse = inverse_factor(gram)

    left = dot_nn(inverse, plane_total(1, copies))
    sent += copies
    gathered[dp] = left
    passing = [send(gathered.at[dp], gathered.at[dp], pass_send.at[0], pass_recv.at[0], sibling)]
    gathering = {}
    for k in sorted(range(1, NZ), key=lambda k: -min(k, NZ - k)):
        gathering[k] = send(
            gathered.at[dp], gathered.at[dp], gather_send.at[k], gather_recv.at[k], along_z(k)
        )
    far_copies = sum_along_z(1, z_term(left))
    for k in sorted(range(1, NZ), key=lambda k: min(k, NZ - k)):
        gathering[k].wait_recv()
        origin = lax.rem(z - k + NZ, NZ) * 2 + core
        passing.append(
            send(gathered.at[origin], gathered.at[origin], pass_send.at[k], pass_recv.at[k], sibling)
        )
    for copy in passing:
        copy.wait_recv()
    sent += passing + list(gathering.values())
    gram = jnp.zeros((RANK, RANK), F32)
    for d in range(2 * NZ):
        gram = gram + dot_nt(gathered[d], gathered[d])
    gram = jnp.concatenate([gram, jnp.zeros((RANK, LANES - RANK), F32)], axis=1)
    inverse = inverse_factor(gram)
    for d in range(2 * NZ):
        orth_ref[d] = dot_nn(inverse, gathered[d])
    z_total(1, far_copies)
    right = jnp.concatenate([halves[1, 0, 0:RANK, :], halves[1, 1, 0:RANK, :]], axis=1)
    right_ref[...] = dot_nn(inverse, right)
    for copy in sent:
        copy.wait_send()


def residual(g_ref, e_ref, orth_ref, right_ref, out_ref):
    block = g_ref.shape[1] // orth_ref.shape[0]
    right = right_ref[...]
    for b in range(orth_ref.shape[0]):
        rows = slice(b * block, (b + 1) * block)
        approx = lax.dot_general(
            orth_ref[b], right, (((0,), (0,)), ((), ())), precision=HIGH, preferred_element_type=F32
        )
        total = g_ref[0, rows, :].astype(F32) + e_ref[0, rows, :].astype(F32)
        out_ref[0, rows, :] = (total - approx[:block]).astype(jnp.bfloat16)


def per_device(gradient, error_in, q_start):
    rows, columns = gradient.shape[1:]
    block = rows // (2 * NZ)
    hbm = pl.BlockSpec(memory_space=pl.ANY)
    vmem = pl.BlockSpec(memory_space=pltpu.VMEM)
    dma = pltpu.SemaphoreType.DMA
    half = RANK + 8
    orth, right = pl.pallas_call(
        compress,
        out_shape=[
            jax.ShapeDtypeStruct((2 * NZ, RANK, LANES), F32),
            jax.ShapeDtypeStruct((RANK, columns), F32),
        ],
        in_specs=[hbm, hbm, vmem],
        out_specs=[vmem, vmem],
        scratch_shapes=[
            pltpu.VMEM((rows, columns), jnp.bfloat16),
            pltpu.VMEM((rows, columns), jnp.bfloat16),
            pltpu.VMEM((NZ, block, columns), F32),
            pltpu.VMEM((NZ, block, columns), F32),
            pltpu.VMEM((NZ, block, columns), F32),
            pltpu.VMEM((2, 8, block, columns), F32),
            pltpu.VMEM((LANES, columns), F32),
            pltpu.VMEM((2, RANK, LANES), F32),
            pltpu.VMEM((2, NT, RANK, LANES), F32),
            pltpu.VMEM((2, 2 * half, LANES), F32),
            pltpu.VMEM((2, half, LANES), F32),
            pltpu.VMEM((2, 4, half, LANES), F32),
            pltpu.VMEM((2, 4, half, LANES), F32),
            pltpu.VMEM((2, 2, half, LANES), F32),
            pltpu.VMEM((2 * NZ, RANK, LANES), F32),
            dma((2,)),
            dma((NZ,)), dma((NZ,)),
            dma((2, 8, CHUNKS)), dma((2, 8, CHUNKS)),
            dma((2, NT)), dma((2, NT)),
            dma((2,)), dma((2,)),
            dma((2, 4)), dma((2, 4)),
            dma((2, 4)), dma((2, 4)),
            dma((2,)), dma((2,)),
            dma((NZ,)), dma((NZ,)),
            dma((NZ,)), dma((NZ,)),
        ],
        compiler_params=pltpu.CompilerParams(
            collective_id=0, has_side_effects=True, vmem_limit_bytes=24 * 2**20
        ),
        name="compress",
    )(gradient, error_in, q_start)
    steps = 4
    tile = rows // steps
    error_out = pl.pallas_call(
        residual,
        grid=(steps,),
        out_shape=jax.ShapeDtypeStruct(gradient.shape, gradient.dtype),
        in_specs=[
            pl.BlockSpec((1, tile, columns), lambda i: (0, i, 0)),
            pl.BlockSpec((1, tile, columns), lambda i: (0, i, 0)),
            pl.BlockSpec((2 * NZ // steps, RANK, LANES), lambda i: (i, 0, 0)),
            pl.BlockSpec((RANK, columns), lambda i: (0, 0)),
        ],
        out_specs=pl.BlockSpec((1, tile, columns), lambda i: (0, i, 0)),
        name="residual",
    )(gradient, error_in, orth, right)
    return (error_out, right)


def solution(mesh):
    placed = (P("dp", None, "tensor"), P("dp", None, "tensor"), P(None, "tensor"))
    return jax.shard_map(
        per_device,
        mesh=mesh,
        in_specs=placed,
        out_specs=(P("dp", None, "tensor"), P(None, "tensor")),
        check_vma=False,
    )
```

time: 711 us -> 101 us (0.14)
  blocking collectives: 480 us -> 0 us
  waiting for transfers between devices: 181 us -> 0 us
  Pallas kernels: 0 us -> 94.3 us
  matrix products: 17.2 us -> 0 us
  between operations: 14.1 us -> 0.66 us
  other arithmetic: 8.03 us -> 0 us
    psum x6 -> x0, blocking collectives: 449 us -> none  [the longest x2 205 us: per_device(): right = lax.psum(right_term, 'dp') / replicas]
    unnamed x4 -> x0, waiting for transfers between devices: 181 us -> none
    pallas_call x0 -> x2, Pallas kernels: none -> 94.3 us  [the longest x1 87.9 us: per_device(): pl.pallas_call(compress, out_shape=[jax.ShapeDtypeStruct((2 * NZ, RANK, L...]
    all_gather x2 -> x0, blocking collectives: 31.2 us -> none  [per_device(): left_orth = lax.all_gather(orth_share, 'tensor', axis=1, tiled=True)]
    dot_general x6 -> x0, matrix products: 13.1 us -> none  [the longest x1 4.88 us: per_device(): lax.dot_general(right, accumulated, (((1,), (1,)), ((), ())), precision=l...]
    another operation x10 -> x0, other arithmetic: 8.01 us -> none  [the longest x6 4.26 us: orthonormal(): lower = jnp.linalg.cholesky(gram)]
  transfers between devices with their start and end apart: 2 -> 0, of which waited for: 2 -> 0; matrix products, arithmetic and copies ran while one was open for 0% -> 0% of each run, Pallas kernels for 0% -> 0%
where the time goes in v1:
time: 101 us; the launch traced here: 100 us
  Pallas kernels  94.3 us (93%)
  local copies, waits for them, and re-layouts  5.44 us (5%)
    pallas_call x1, Pallas kernels, per_device(): pl.pallas_call(compress, out_shape=[jax.ShapeDtypeStruct((2 * NZ, RANK, L...  87.9 us
    pallas_call x1, Pallas kernels, per_device(): pl.pallas_call(residual, grid=(steps,), out_shape=jax.ShapeDtypeStruct(gr...  6.38 us
    unnamed x13, local copies, waits for them, and re-layouts  5.44 us

profile of v1, /device:TPU:1, one launch (start us, length us, event | category | flops | bytes accessed | tf_op | source)
XLA Modules:
  0.0 100.4 jit_solution(8959822978262263668)
XLA Ops:
  0.6 0.0 copy-start
  0.6 1.4 %copy-done = bf16[1,3072,256]{2,1,0:T(8,128)(2,1)S(1)} copy-done((bf16[1,3072,256]{2,1,0:T(8,128)(2,1)S(1)}, bf16[1,3072,256]{2,1,0:T(8,128)(2,1)}, u32[]{:S(2)}) %copy-start) | copy-done | bytes 1572888
  2.0 0.0 copy-start.1
  2.0 1.4 %copy-done.1 = bf16[1,3072,256]{2,1,0:T(8,128)(2,1)S(1)} copy-done((bf16[1,3072,256]{2,1,0:T(8,128)(2,1)S(1)}, bf16[1,3072,256]{2,1,0:T(8,128)(2,1)}, u32[]{:S(2)}) %copy-start.1) | copy-done | bytes 1572888
  3.4 0.0 copy-start.5
  3.5 0.7 copy-done.5
  4.2 87.9 %compress.1 = (f32[32,16,128]{2,1,0:T(8,128)S(1)}, f32[16,256]{1,0:T(8,128)S(1)}) custom-call(bf16[1,3072,256]{2,1,0:T(8,128)(2,1)S(1)} %copy-done, bf16[1,3072,256]{2,1,0:T(8,128)(2,1)S(1)} %copy-done.1, f32[16,256]{1,0:T(8,128)S(1)} %copy-done.5), custom_call_target="tpu_custom_call" | custom-call | tf_op jit(solution)/shard_map/compress/pallas_call | solution.py:291
  92.1 0.0 copy-start.2
  92.1 0.7 copy-done.2
  92.8 0.0 copy-start.3
  92.8 0.6 copy-done.3
  93.4 0.0 copy-start.4
  93.4 6.4 %residual.1 = bf16[1,3072,256]{2,1,0:T(8,128)(2,1)} custom-call(bf16[1,3072,256]{2,1,0:T(8,128)(2,1)} %g_ref.1, bf16[1,3072,256]{2,1,0:T(8,128)(2,1)} %e_ref.1, f32[32,16,128]{2,1,0:T(8,128)} %copy-done.2, f32[16,256]{1,0:T(8,128)} %copy-done.3), custom_call_target="tpu_custom_call" | custom-call | tf_op jit(solution)/shard_map/residual/pallas_call | solution.py:333
  99.8 0.0 copy-done.4
  99.8 0.6 copy.6
Async XLA Ops:
  0.6 1.4 %copy-start = (bf16[1,3072,256]{2,1,0:T(8,128)(2,1)S(1)}, bf16[1,3072,256]{2,1,0:T(8,128)(2,1)}, u32[]{:S(2)}) copy-start(bf16[1,3072,256]{2,1,0:T(8,128)(2,1)} %g_ref.1) | copy-start | bytes 4718596
  2.0 1.4 %copy-start.1 = (bf16[1,3072,256]{2,1,0:T(8,128)(2,1)S(1)}, bf16[1,3072,256]{2,1,0:T(8,128)(2,1)}, u32[]{:S(2)}) copy-start(bf16[1,3072,256]{2,1,0:T(8,128)(2,1)} %e_ref.1) | copy-start | bytes 4718596
  3.4 0.7 copy-start.5
  92.1 0.7 copy-start.2
  92.8 0.6 copy-start.3
  93.4 6.4 %copy-start.4 = (f32[16,256]{1,0:T(8,128)S(1)}, f32[16,256]{1,0:T(8,128)}, u32[]{:S(2)}) copy-start(f32[16,256]{1,0:T(8,128)} %copy-done.3) | copy-start | bytes 49156

commit v2 on v1

v2 whole, which is shorter than its diff:
```python
import jax
import jax.numpy as jnp
from jax import lax
from jax.experimental import pallas as pl
from jax.experimental.pallas import tpu as pltpu
from jax.sharding import PartitionSpec as P

MESH = pl.DeviceIdType.MESH
F32 = jnp.float32
HIGH = lax.Precision.HIGHEST

RANK = 16
LANES = 128
NZ = 16
NT = 16
CHUNKS = 4


def dot_nn(a, b):
    return lax.dot_general(a, b, (((1,), (0,)), ((), ())), precision=HIGH, preferred_element_type=F32)


def dot_nt(a, b):
    return lax.dot_general(a, b, (((1,), (1,)), ((), ())), precision=HIGH, preferred_element_type=F32)


def inverse_factor(gram):
    rows = lax.broadcasted_iota(jnp.int32, (RANK, LANES), 0)
    lanes = lax.broadcasted_iota(jnp.int32, (RANK, LANES), 1)
    both = gram + (lanes == rows + RANK).astype(F32)
    for j in range(RANK):
        column = both[:, j : j + 1]
        scale = 1.0 / jnp.sqrt(column[j : j + 1, :])
        pivot = both[j : j + 1, :] * scale
        step = both - (column * scale) * pivot
        both = jnp.where(rows == j, pivot, jnp.where(rows > j, step, both))
    return both[:, RANK : 2 * RANK]


def split_three(value):
    top = value.astype(jnp.bfloat16)
    rest = value - top.astype(F32)
    middle = rest.astype(jnp.bfloat16)
    return top, middle, (rest - middle.astype(F32)).astype(jnp.bfloat16)


def compress(
    g_hbm, e_hbm, q_ref, out_ref, right_ref,
    g_ref, e_ref, own, cross, cross_in, ring, mean, share, shares, term, pair, near, far, halves, relay, gathered,
    load_sem, cross_send, cross_recv, ring_send, ring_recv, share_send, share_recv,
    pair_send, pair_recv, near_send, near_recv, far_send, far_recv, half_send, half_recv,
    relay_send, relay_recv, gather_send, gather_recv, pass_send, pass_recv, known_one, known_two,
):
    dp, tensor = lax.axis_index("dp"), lax.axis_index("tensor")
    z, core = dp // 2, dp % 2
    x, y = tensor // 4, tensor % 4
    block = own.shape[1]
    other = 1 - core

    up = [lax.rem(z + 8 - k, NZ) for k in range(8)]
    down = [lax.rem(z + 9 + k, NZ) for k in range(7)]
    order = []
    for k in range(8):
        order.append(up[k])
        if k < 7:
            order.append(down[k])
    order.append(z)

    loads = []
    for i, j in enumerate(order):
        rows = pl.ds(pl.multiple_of(j * (2 * block), 2 * block), 2 * block)
        loads.append(
            (
                pltpu.make_async_copy(g_hbm.at[0, rows], g_ref.at[rows], load_sem.at[0, i]),
                pltpu.make_async_copy(e_hbm.at[0, rows], e_ref.at[rows], load_sem.at[1, i]),
            )
        )
        for load in loads[i]:
            load.start()

    sibling = (z * 2 + other, tensor)

    def along_z(hops):
        return (lax.rem(z + hops + NZ, NZ) * 2 + core, tensor)

    def in_plane(k):
        return (dp, lax.rem(tensor + k, NT))

    def hop(dx, dy):
        return (dp, lax.rem(x + dx + 4, 4) * 4 + lax.rem(y + dy + 4, 4))

    steps = [hop(1, 0), hop(-1, 0), hop(0, 1), hop(0, -1)]
    neighbours = [sibling, along_z(1), along_z(-1)] + steps
    barrier = pltpu.get_barrier_semaphore()
    for device in neighbours:
        pl.semaphore_signal(barrier, inc=1, device_id=device, device_id_type=MESH)
    mean[...] = jnp.zeros_like(mean)
    pl.semaphore_wait(barrier, len(neighbours))
    for device in steps:
        pl.semaphore_signal(known_one, inc=1, device_id=device, device_id_type=MESH)

    sent = []

    def send(src, dst, send_sem, recv_sem, device):
        copy = pltpu.make_async_remote_copy(
            src_ref=src, dst_ref=dst, send_sem=send_sem, recv_sem=recv_sem, device_id=device, device_id_type=MESH
        )
        copy.start()
        sent.append(copy)
        return copy

    def accumulated(index):
        rows = pl.ds(pl.multiple_of(index * block, block), block)
        return g_ref[rows, :].astype(F32) + e_ref[rows, :].astype(F32)

    part = block // CHUNKS

    def forward(direction, k, target, c):
        rows = pl.ds(c * part, part)
        return send(
            own.at[target, rows], ring.at[direction, k, rows],
            ring_send.at[direction, k, c], ring_recv.at[direction, k, c],
            along_z(1 if direction == 0 else -1),
        )

    crossing = []

    def cross_over(i):
        for load in loads[i]:
            load.wait()
        cross[i] = accumulated(2 * order[i] + other)
        crossing.append(send(cross.at[i], cross_in.at[i], cross_send.at[i], cross_recv.at[i], sibling))

    def add_cores(i):
        mine = accumulated(2 * order[i] + core)
        crossing[i].wait_recv()
        own[order[i]] = mine + cross_in[i]

    cross_over(0)
    cross_over(1)
    cross_over(2)
    cross_over(3)
    add_cores(0)
    ring_up = [forward(0, 0, up[0], c) for c in range(CHUNKS)]
    add_cores(1)
    ring_down = [forward(1, 0, down[0], c) for c in range(CHUNKS)]
    for i in range(4, 16):
        cross_over(i)
    for i in range(2, 16):
        add_cores(i)

    def take(copies, direction, k, target, c, onward):
        rows = pl.ds(c * part, part)
        copies[c].wait_recv()
        own[target, rows, :] = own[target, rows, :] + ring[direction, k, rows, :]
        if onward:
            copies[c] = forward(direction, k + 1, target, c)

    for k in range(1, 9):
        for c in range(CHUNKS):
            take(ring_up, 0, k - 1, up[k] if k < 8 else z, c, k < 8)
            if k < 8:
                take(ring_down, 1, k - 1, down[k] if k < 7 else z, c, k < 7)
        if k == 2:
            pl.semaphore_wait(known_one, len(steps))
            for device in [hop(2, 0), hop(0, 2), hop(1, 1), hop(1, -1), hop(-1, 1), hop(-1, -1)]:
                pl.semaphore_signal(known_two, inc=1, device_id=device, device_id_type=MESH)
    pl.semaphore_wait(known_two, 6)
    mean[0:block, :] = own[z] * (1.0 / 32.0)

    def sum_in_plane(sweep, value):
        share[sweep] = value
        copies = []
        for k in range(1, NT):
            copies.append(
                send(
                    share.at[sweep], shares.at[sweep, tensor],
                    share_send.at[sweep, k], share_recv.at[sweep, k], in_plane(k),
                )
            )
        shares[sweep, tensor] = value
        return copies

    def plane_total(sweep, copies):
        for copy in copies:
            copy.wait_recv()
        total = shares[sweep, 0]
        for k in range(1, NT):
            total = total + shares[sweep, k]
        return total

    group, place = z // 4, z % 4

    def sum_near(sweep, value):
        half = value.shape[0] // 2
        term[sweep, 0 : 2 * half, :] = value
        kept = pl.ds(0, half)
        swap = send(
            term.at[sweep, pl.ds(other * half, half)], pair.at[sweep, kept],
            pair_send.at[sweep], pair_recv.at[sweep], sibling,
        )
        swap.wait_recv()
        near[sweep, place, kept, :] = term[sweep, pl.ds(core * half, half), :] + pair[sweep, kept, :]
        copies = []
        for k in range(1, 4):
            device = ((group * 4 + (place + k) % 4) * 2 + core, tensor)
            copies.append(
                send(
                    near.at[sweep, place, kept], near.at[sweep, place, kept],
                    near_send.at[sweep, k], near_recv.at[sweep, k], device,
                )
            )
        for copy in copies:
            copy.wait_recv()
        far[sweep, group, kept, :] = (
            near[sweep, 0, kept, :] + near[sweep, 1, kept, :] + near[sweep, 2, kept, :] + near[sweep, 3, kept, :]
        )
        copies = []
        for k in (2, 1, 3):
            copies.append(
                send(
                    far.at[sweep, group, kept], far.at[sweep, group, kept],
                    far_send.at[sweep, k], far_recv.at[sweep, k], along_z(4 * k),
                )
            )
        return copies

    def sum_far(sweep, half, copies):
        kept = pl.ds(0, half)
        for copy in copies:
            copy.wait_recv()
        halves[sweep, core, kept, :] = (
            far[sweep, 0, kept, :] + far[sweep, 1, kept, :] + far[sweep, 2, kept, :] + far[sweep, 3, kept, :]
        )
        return send(
            halves.at[sweep, core, kept], halves.at[sweep, core, kept],
            half_send.at[sweep], half_recv.at[sweep], sibling,
        )

    pad = jnp.zeros((RANK, LANES - RANK), F32)

    copies = sum_in_plane(0, dot_nt(q_ref[...], mean[...]))
    left = plane_total(0, copies)
    wide = dot_nn(left, mean[...])
    gram = jnp.concatenate([dot_nt(left, left), pad], axis=1)
    value = jnp.concatenate([wide[:, :LANES], gram[:8], wide[:, LANES:], gram[8:]], axis=0)
    sum_far(0, RANK + 8, sum_near(0, value)).wait_recv()
    right = jnp.concatenate([halves[0, 0, 0:RANK, :], halves[0, 1, 0:RANK, :]], axis=1)
    copies = sum_in_plane(1, dot_nt(right, mean[...]))
    gram = jnp.concatenate([halves[0, 0, RANK : RANK + 8, :], halves[0, 1, RANK : RANK + 8, :]], axis=0)
    inverse = inverse_factor(gram)

    left = dot_nn(inverse, plane_total(1, copies))
    gathered[dp] = left

    def relayed():
        return pltpu.make_async_remote_copy(
            src_ref=gathered.at[dp], dst_ref=relay, send_sem=relay_send, recv_sem=relay_recv,
            device_id=along_z(tensor), device_id_type=MESH,
        )

    @pl.when(tensor > 0)
    def _():
        relayed().start()

    def hand_done():
        @pl.when(tensor > 0)
        def _():
            for k in range(1, NT):
                handed(k).wait_send()

    passing = [send(gathered.at[dp], gathered.at[dp], pass_send.at[0], pass_recv.at[0], sibling)]
    wide = dot_nn(left, mean[...])
    far_copies = sum_near(1, jnp.concatenate([wide[:, :LANES], wide[:, LANES:]], axis=0))

    origin = lax.rem(z - tensor + NZ, NZ) * 2 + core

    def handed(k):
        return pltpu.make_async_remote_copy(
            src_ref=relay, dst_ref=gathered.at[origin], send_sem=gather_send.at[k],
            recv_sem=gather_recv.at[tensor], device_id=in_plane(k), device_id_type=MESH,
        )

    @pl.when(tensor > 0)
    def _():
        relayed().wait()
        for k in range(1, NT):
            handed(k).start()
        gathered[origin] = relay[...]

    for k in range(1, NT):
        source = lax.rem(z - k + NZ, NZ) * 2 + core

        @pl.when(tensor != k)
        def _():
            pltpu.make_async_remote_copy(
                src_ref=relay, dst_ref=gathered.at[source], send_sem=gather_send.at[k],
                recv_sem=gather_recv.at[k], device_id=in_plane(k), device_id_type=MESH,
            ).wait_recv()

        passing.append(
            send(gathered.at[source], gathered.at[source], pass_send.at[k], pass_recv.at[k], sibling)
        )
    for copy in passing:
        copy.wait_recv()
    gram = jnp.zeros((RANK, RANK), F32)
    for d in range(2 * NZ):
        gram = gram + dot_nt(gathered[d], gathered[d])
    inverse = inverse_factor(jnp.concatenate([gram, pad], axis=1))
    last = sum_far(1, RANK, far_copies)
    tops, middles, lows = [], [], []
    for d in range(2 * NZ):
        orth = dot_nn(inverse, gathered[d])
        top, middle, low = split_three(orth)
        tops.append(jnp.concatenate([top, middle, top, low, middle, top], axis=0))
    last.wait_recv()
    right = dot_nn(inverse, jnp.concatenate([halves[1, 0, 0:RANK, :], halves[1, 1, 0:RANK, :]], axis=1))
    right_ref[...] = right
    top, middle, low = split_three(right)
    stacked = jnp.concatenate([top, top, middle, top, middle, low], axis=0)
    for d in range(2 * NZ):
        rows = pl.ds(d * block, block)
        approx = lax.dot_general(tops[d], stacked, (((0,), (0,)), ((), ())), preferred_element_type=F32)
        total = g_ref[rows, :].astype(F32) + e_ref[rows, :].astype(F32)
        out_ref[0, rows, :] = (total - approx[:block]).astype(jnp.bfloat16)

    hand_done()
    for copy in sent:
        copy.wait_send()


def per_device(gradient, error_in, q_start):
    rows, columns = gradient.shape[1:]
    block = rows // (2 * NZ)
    hbm = pl.BlockSpec(memory_space=pltpu.HBM)
    vmem = pl.BlockSpec(memory_space=pltpu.VMEM)
    dma = pltpu.SemaphoreType.DMA
    half = RANK + 8
    return pl.pallas_call(
        compress,
        out_shape=[
            jax.ShapeDtypeStruct(gradient.shape, gradient.dtype),
            jax.ShapeDtypeStruct((RANK, columns), F32),
        ],
        in_specs=[hbm, hbm, vmem],
        out_specs=[vmem, vmem],
        scratch_shapes=[
            pltpu.VMEM((rows, columns), jnp.bfloat16),
            pltpu.VMEM((rows, columns), jnp.bfloat16),
            pltpu.VMEM((NZ, block, columns), F32),
            pltpu.VMEM((NZ, block, columns), F32),
            pltpu.VMEM((NZ, block, columns), F32),
            pltpu.VMEM((2, 8, block, columns), F32),
            pltpu.VMEM((LANES, columns), F32),
            pltpu.VMEM((2, RANK, LANES), F32),
            pltpu.VMEM((2, NT, RANK, LANES), F32),
            pltpu.VMEM((2, 2 * half, LANES), F32),
            pltpu.VMEM((2, half, LANES), F32),
            pltpu.VMEM((2, 4, half, LANES), F32),
            pltpu.VMEM((2, 4, half, LANES), F32),
            pltpu.VMEM((2, 2, half, LANES), F32),
            pltpu.VMEM((RANK, LANES), F32),
            pltpu.VMEM((2 * NZ, RANK, LANES), F32),
            dma((2, NZ)),
            dma((NZ,)), dma((NZ,)),
            dma((2, 8, CHUNKS)), dma((2, 8, CHUNKS)),
            dma((2, NT)), dma((2, NT)),
            dma((2,)), dma((2,)),
            dma((2, 4)), dma((2, 4)),
            dma((2, 4)), dma((2, 4)),
            dma((2,)), dma((2,)),
            dma, dma,
            dma((NT,)), dma((NT,)),
            dma((NZ,)), dma((NZ,)),
            pltpu.SemaphoreType.REGULAR, pltpu.SemaphoreType.REGULAR,
        ],
        compiler_params=pltpu.CompilerParams(
            collective_id=0, has_side_effects=True, vmem_limit_bytes=52 * 2**20
        ),
        name="compress",
    )(gradient, error_in, q_start)


def solution(mesh):
    placed = (P("dp", None, "tensor"), P("dp", None, "tensor"), P(None, "tensor"))
    return jax.shard_map(
        per_device,
        mesh=mesh,
        in_specs=placed,
        out_specs=(P("dp", None, "tensor"), P(None, "tensor")),
        check_vma=False,
    )
```

time: 101 us -> 88.9 us (0.88)
  Pallas kernels: 94.3 us -> 85.6 us
  local copies, waits for them, and re-layouts: 5.44 us -> 2.46 us
    pallas_call x2 -> x1, Pallas kernels: 94.3 us -> 85.6 us  [per_device(): pl.pallas_call(compress, out_shape=[jax.ShapeDtypeStruct(gradient.shape,...]
    unnamed x13 -> x4, local copies, waits for them, and re-layouts: 5.44 us -> 2.46 us
where the time goes in v2:
time: 88.9 us; the launch traced here: 88.7 us
  Pallas kernels  85.6 us (96%)
  local copies, waits for them, and re-layouts  2.46 us (3%)
    pallas_call x1, Pallas kernels, per_device(): pl.pallas_call(compress, out_shape=[jax.ShapeDtypeStruct(gradient.shape,...  85.6 us
    unnamed x4, local copies, waits for them, and re-layouts  2.46 us

profile of v2, /device:TPU:1, one launch (start us, length us, event | category | flops | bytes accessed | tf_op | source)
XLA Modules:
  0.0 88.7 jit_solution(9298441836226616698)
XLA Ops:
  0.6 0.0 copy-start
  0.6 0.7 copy-done
  1.3 85.6 %compress.1 = (bf16[1,3072,256]{2,1,0:T(8,128)(2,1)S(1)}, f32[16,256]{1,0:T(8,128)S(1)}) custom-call(bf16[1,3072,256]{2,1,0:T(8,128)(2,1)} %g_hbm.1, bf16[1,3072,256]{2,1,0:T(8,128)(2,1)} %e_hbm.1, f32[16,256]{1,0:T(8,128)S(1)} %copy-done), custom_call_target="tpu_custom_call" | custom-call | tf_op jit(solution)/shard_map/compress/pallas_call | solution.py:339
  87.0 1.1 %copy.7 = bf16[1,3072,256]{2,1,0:T(8,128)(2,1)} copy(bf16[1,3072,256]{2,1,0:T(8,128)(2,1)S(1)} %get-tuple-element.4) | data formatting | bytes 3145728
  88.1 0.6 copy.8
Async XLA Ops:
  0.6 0.7 copy-start

commit v3 on v2

--- a/solution.py
+++ b/solution.py
@@ -45,15 +45,17 @@
 
 
 def compress(
-    g_hbm, e_hbm, q_ref, out_ref, right_ref,
-    g_ref, e_ref, own, cross, cross_in, ring, mean, share, shares, term, pair, near, far, halves, relay, gathered,
+    g_hbm, e_hbm, q_hbm, out_ref, right_ref,
+    g_ref, e_ref, q_ref, early, early_in, early_sum, plane_in, first, own, cross, cross_in, ring, mean_top, mean_middle, mean_low, share, shares, term, pair, near, far, halves, relay, gathered, turned,
     load_sem, cross_send, cross_recv, ring_send, ring_recv, share_send, share_recv,
     pair_send, pair_recv, near_send, near_recv, far_send, far_recv, half_send, half_recv,
-    relay_send, relay_recv, gather_send, gather_recv, pass_send, pass_recv, known_one, known_two,
+    early_send, early_recv, plane_send, plane_recv, owner_send, owner_recv, q_sem,
+    relay_send, relay_recv, gather_send, gather_recv, pass_send, pass_recv, known_one, known_two, known_z,
 ):
     dp, tensor = lax.axis_index("dp"), lax.axis_index("tensor")
     z, core = dp // 2, dp % 2
     x, y = tensor // 4, tensor % 4
+    mean_parts = (mean_top, mean_middle, mean_low)
     block = own.shape[1]
     other = 1 - core
 
@@ -66,6 +68,7 @@
             order.append(down[k])
     order.append(z)
 
+    q_load = pltpu.make_async_copy(q_hbm, q_ref, q_sem)
     loads = []
     for i, j in enumerate(order):
         rows = pl.ds(pl.multiple_of(j * (2 * block), 2 * block), 2 * block)
@@ -77,6 +80,8 @@
         )
         for load in loads[i]:
             load.start()
+        if i == 1:
+            q_load.start()
 
     sibling = (z * 2 + other, tensor)
 
@@ -94,10 +99,31 @@
     barrier = pltpu.get_barrier_semaphore()
     for device in neighbours:
         pl.semaphore_signal(barrier, inc=1, device_id=device, device_id_type=MESH)
-    mean[...] = jnp.zeros_like(mean)
+    for part_ref in mean_parts:
+        part_ref[...] = jnp.zeros_like(part_ref)
+    early[...] = jnp.zeros_like(early)
+    early_sum[...] = jnp.zeros_like(early_sum)
+
+    def accumulated(index):
+        rows = pl.ds(pl.multiple_of(index * block, block), block)
+        return g_ref[rows, :].astype(F32) + e_ref[rows, :].astype(F32)
+
+    def wait_load(i):
+        for load in loads[i]:
+            load.wait()
+
+    for i in range(4):
+        wait_load(i)
+        cross[i] = accumulated(2 * order[i] + other)
     pl.semaphore_wait(barrier, len(neighbours))
-    for device in steps:
-        pl.semaphore_signal(known_one, inc=1, device_id=device, device_id_type=MESH)
+
+    def tell(semaphore, devices):
+        for device in devices:
+            pl.semaphore_signal(semaphore, inc=1, device_id=device, device_id_type=MESH)
+
+    corners = [hop(2, 0), hop(0, 2), hop(1, 1), hop(1, -1), hop(-1, 1), hop(-1, -1)]
+    tell(known_one, steps)
+    tell(known_z.at[0], [along_z(1), along_z(-1)])
 
     sent = []
 
@@ -108,10 +134,6 @@
         copy.start()
         sent.append(copy)
         return copy
-
-    def accumulated(index):
-        rows = pl.ds(pl.multiple_of(index * block, block), block)
-        return g_ref[rows, :].astype(F32) + e_ref[rows, :].astype(F32)
 
     part = block // CHUNKS
 
@@ -126,9 +148,8 @@
     crossing = []
 
     def cross_over(i):
-        for load in loads[i]:
-            load.wait()
-        cross[i] = accumulated(2 * order[i] + other)
+        if i >= 4:
+            cross[i] = accumulated(2 * order[i] + other)
         crossing.append(send(cross.at[i], cross_in.at[i], cross_send.at[i], cross_recv.at[i], sibling))
 
     def add_cores(i):
@@ -136,18 +157,38 @@
         crossing[i].wait_recv()
         own[order[i]] = mine + cross_in[i]
 
-    cross_over(0)
-    cross_over(1)
-    cross_over(2)
-    cross_over(3)
+    for i in range(4):
+        cross_over(i)
+    q_load.wait()
+    q_parts = jnp.concatenate(split_three(q_ref[...]), axis=0)
+
+    def early_term(j):
+        for half in range(2):
+            rows = pl.ds(pl.multiple_of((2 * j + half) * block, block), block)
+            dims = (((1,), (1,)), ((), ()))
+            three = lax.dot_general(q_parts, g_ref[rows, :], dims, preferred_element_type=F32)
+            three = three + lax.dot_general(q_parts, e_ref[rows, :], dims, preferred_element_type=F32)
+            early[j, half, :, 0:block] = three[:RANK] + (three[RANK : 2 * RANK] + three[2 * RANK :])
+
+    for i in range(0, 4):
+        early_term(order[i])
     add_cores(0)
     ring_up = [forward(0, 0, up[0], c) for c in range(CHUNKS)]
     add_cores(1)
     ring_down = [forward(1, 0, down[0], c) for c in range(CHUNKS)]
+    for i in range(4, 8):
+        wait_load(i)
+        cross_over(i)
+    for i in range(8, 16):
+        wait_load(i)
     for i in range(4, 16):
-        cross_over(i)
-    for i in range(2, 16):
-        add_cores(i)
+        early_term(order[i])
+    add_cores(2)
+    add_cores(3)
+    pl.semaphore_wait(known_one, len(steps))
+    pl.semaphore_wait(known_z.at[0], 2)
+    tell(known_two, corners)
+    tell(known_z.at[1], [along_z(2), along_z(-2)])
 
     def take(copies, direction, k, target, c, onward):
         rows = pl.ds(c * part, part)
@@ -156,37 +197,116 @@
         if onward:
             copies[c] = forward(direction, k + 1, target, c)
 
+    def to_owner(half):
+        return pltpu.make_async_remote_copy(
+            src_ref=early_sum.at[half], dst_ref=plane_in.at[dp], send_sem=plane_send.at[half],
+            recv_sem=plane_recv.at[dp], device_id=(2 * tensor + half, tensor), device_id_type=MESH,
+        )
+
+    def from_owner(n):
+        return pltpu.make_async_remote_copy(
+            src_ref=first, dst_ref=first, send_sem=owner_send.at[n], recv_sem=owner_recv,
+            device_id=in_plane(n), device_id_type=MESH,
+        )
+
+    def early_done():
+        for half in range(2):
+
+            @pl.when(dp != 2 * tensor + half)
+            def _():
+                to_owner(half).wait_send()
+
+        @pl.when(z == tensor)
+        def _():
+            for n in range(1, NT):
+                from_owner(n).wait_send()
+
     for k in range(1, 9):
         for c in range(CHUNKS):
             take(ring_up, 0, k - 1, up[k] if k < 8 else z, c, k < 8)
             if k < 8:
                 take(ring_down, 1, k - 1, down[k] if k < 7 else z, c, k < 7)
+        for i in range(2 * k + 6, min(2 * k + 8, 16)):
+            cross_over(i)
+        for i in range(2 * k + 2, min(2 * k + 4, 16)):
+            add_cores(i)
+        if k == 1:
+            pl.semaphore_wait(known_two, len(corners))
+            pl.semaphore_wait(known_z.at[1], 2)
+            tell(known_z.at[2], [along_z(4), along_z(-4)])
+            early_copies = []
+            for n in range(1, NT):
+                early_copies.append(
+                    send(
+                        early.at[lax.rem(tensor + n, NT)], early_in.at[n],
+                        early_send.at[n], early_recv.at[n], in_plane(n),
+                    )
+                )
         if k == 2:
-            pl.semaphore_wait(known_one, len(steps))
-            for device in [hop(2, 0), hop(0, 2), hop(1, 1), hop(1, -1), hop(-1, 1), hop(-1, -1)]:
-                pl.semaphore_signal(known_two, inc=1, device_id=device, device_id_type=MESH)
-    pl.semaphore_wait(known_two, 6)
-    mean[0:block, :] = own[z] * (1.0 / 32.0)
-
-    def sum_in_plane(sweep, value):
-        share[sweep] = value
+            pl.semaphore_wait(known_z.at[2], 2)
+            tell(known_z.at[3], [sibling])
+        if k == 3:
+            pl.semaphore_wait(known_z.at[3], 1)
+            total = early[tensor]
+            for n in range(1, NT):
+                early_copies[n - 1].wait_recv()
+                total = total + early_in[n]
+            early_sum[...] = total
+            for half in range(2):
+
+                @pl.when(dp != 2 * tensor + half)
+                def _():
+                    to_owner(half).start()
+
+                @pl.when(dp == 2 * tensor + half)
+                def _():
+                    plane_in[dp] = early_sum[half]
+        if k == 6:
+
+            @pl.when(z == tensor)
+            def _():
+                for source in range(2 * NZ):
+
+                    @pl.when(dp != source)
+                    def _():
+                        pltpu.make_async_remote_copy(
+                            src_ref=early_sum.at[0], dst_ref=plane_in.at[source], send_sem=plane_send.at[0],
+                            recv_sem=plane_recv.at[source], device_id=sibling, device_id_type=MESH,
+                        ).wait_recv()
+
+                total = plane_in[0]
+                for source in range(1, 2 * NZ):
+                    total = total + plane_in[source]
+                first[...] = total * (1.0 / 32.0)
+                for n in range(1, NT):
+                    from_owner(n).start()
+
+    @pl.when(z != tensor)
+    def _():
+        from_owner(1).wait_recv()
+
+    for part_ref, value in zip(mean_parts, split_three(own[z] * (1.0 / 32.0))):
+        part_ref[0:block, :] = value
+
+    def sum_in_plane(value):
+        share[...] = value
         copies = []
         for k in range(1, NT):
             copies.append(
                 send(
-                    share.at[sweep], shares.at[sweep, tensor],
-                    share_send.at[sweep, k], share_recv.at[sweep, k], in_plane(k),
+                    share, shares.at[tensor],
+                    share_send.at[k], share_recv.at[k], in_plane(k),
                 )
             )
-        shares[sweep, tensor] = value
+        shares[tensor] = value
         return copies
 
-    def plane_total(sweep, copies):
+    def plane_total(copies):
         for copy in copies:
             copy.wait_recv()
-        total = shares[sweep, 0]
+        total = shares[0]
         for k in range(1, NT):
-            total = total + shares[sweep, k]
+            total = total + shares[k]
         return total
 
     group, place = z // 4, z % 4
@@ -239,19 +359,28 @@
 
     pad = jnp.zeros((RANK, LANES - RANK), F32)
 
-    copies = sum_in_plane(0, dot_nt(q_ref[...], mean[...]))
-    left = plane_total(0, copies)
-    wide = dot_nn(left, mean[...])
+    def product(value, contract):
+        stacked = jnp.concatenate(split_three(value), axis=0)
+        dims = (((1,), (contract,)), ((), ()))
+        by_top = lax.dot_general(stacked, mean_top[...], dims, preferred_element_type=F32)
+        by_middle = lax.dot_general(stacked[: 2 * RANK], mean_middle[...], dims, preferred_element_type=F32)
+        by_low = lax.dot_general(stacked[:RANK], mean_low[...], dims, preferred_element_type=F32)
+        small = by_top[2 * RANK :] + by_middle[RANK:] + by_low
+        return by_top[:RANK] + ((by_top[RANK : 2 * RANK] + by_middle[:RANK]) + small)
+
+    left = first[...]
+    wide = product(left, 0)
     gram = jnp.concatenate([dot_nt(left, left), pad], axis=1)
     value = jnp.concatenate([wide[:, :LANES], gram[:8], wide[:, LANES:], gram[8:]], axis=0)
     sum_far(0, RANK + 8, sum_near(0, value)).wait_recv()
     right = jnp.concatenate([halves[0, 0, 0:RANK, :], halves[0, 1, 0:RANK, :]], axis=1)
-    copies = sum_in_plane(1, dot_nt(right, mean[...]))
+    copies = sum_in_plane(product(right, 1))
     gram = jnp.concatenate([halves[0, 0, RANK : RANK + 8, :], halves[0, 1, RANK : RANK + 8, :]], axis=0)
     inverse = inverse_factor(gram)
 
-    left = dot_nn(inverse, plane_total(1, copies))
-    gathered[dp] = left
+    left = dot_nn(inverse, plane_total(copies))
+    behind = jnp.concatenate([jnp.zeros((block, LANES), F32), left, jnp.zeros((LANES - block - RANK, LANES), F32)], axis=0)
+    gathered[dp] = left + dot_nt(left, behind)
 
     def relayed():
         return pltpu.make_async_remote_copy(
@@ -270,7 +399,7 @@
                 handed(k).wait_send()
 
     passing = [send(gathered.at[dp], gathered.at[dp], pass_send.at[0], pass_recv.at[0], sibling)]
-    wide = dot_nn(left, mean[...])
+    wide = product(left, 0)
     far_copies = sum_near(1, jnp.concatenate([wide[:, :LANES], wide[:, LANES:]], axis=0))
 
     origin = lax.rem(z - tensor + NZ, NZ) * 2 + core
@@ -288,6 +417,11 @@
             handed(k).start()
         gathered[origin] = relay[...]
 
+    def turn(index):
+        top, middle, low = split_three(gathered[index])
+        turned[index] = jnp.concatenate([top, middle, top, low, middle, top], axis=0).T
+
+    turn(dp)
     for k in range(1, NT):
         source = lax.rem(z - k + NZ, NZ) * 2 + core
 
@@ -301,29 +435,28 @@
         passing.append(
             send(gathered.at[source], gathered.at[source], pass_send.at[k], pass_recv.at[k], sibling)
         )
-    for copy in passing:
+        turn(source)
+    for k, copy in enumerate(passing):
         copy.wait_recv()
-    gram = jnp.zeros((RANK, RANK), F32)
-    for d in range(2 * NZ):
-        gram = gram + dot_nt(gathered[d], gathered[d])
-    inverse = inverse_factor(jnp.concatenate([gram, pad], axis=1))
+        turn(lax.rem(z - k + NZ, NZ) * 2 + other)
+    gram = gathered[0]
+    for d in range(1, 2 * NZ):
+        gram = gram + gathered[d]
+    inverse = inverse_factor(pltpu.roll(gram, LANES - block, 1))
     last = sum_far(1, RANK, far_copies)
-    tops, middles, lows = [], [], []
-    for d in range(2 * NZ):
-        orth = dot_nn(inverse, gathered[d])
-        top, middle, low = split_three(orth)
-        tops.append(jnp.concatenate([top, middle, top, low, middle, top], axis=0))
     last.wait_recv()
     right = dot_nn(inverse, jnp.concatenate([halves[1, 0, 0:RANK, :], halves[1, 1, 0:RANK, :]], axis=1))
     right_ref[...] = right
-    top, middle, low = split_three(right)
+    weights = lax.dot_general(inverse, right, (((0,), (0,)), ((), ())), precision=HIGH, preferred_element_type=F32)
+    top, middle, low = split_three(weights)
     stacked = jnp.concatenate([top, top, middle, top, middle, low], axis=0)
     for d in range(2 * NZ):
         rows = pl.ds(d * block, block)
-        approx = lax.dot_general(tops[d], stacked, (((0,), (0,)), ((), ())), preferred_element_type=F32)
+        approx = jnp.dot(turned[d], stacked, preferred_element_type=F32)
         total = g_ref[rows, :].astype(F32) + e_ref[rows, :].astype(F32)
         out_ref[0, rows, :] = (total - approx[:block]).astype(jnp.bfloat16)
 
+    early_done()
     hand_done()
     for copy in sent:
         copy.wait_send()
@@ -342,18 +475,26 @@
             jax.ShapeDtypeStruct(gradient.shape, gradient.dtype),
             jax.ShapeDtypeStruct((RANK, columns), F32),
         ],
-        in_specs=[hbm, hbm, vmem],
+        in_specs=[hbm, hbm, hbm],
         out_specs=[vmem, vmem],
         scratch_shapes=[
             pltpu.VMEM((rows, columns), jnp.bfloat16),
             pltpu.VMEM((rows, columns), jnp.bfloat16),
+            pltpu.VMEM((RANK, columns), F32),
+            pltpu.VMEM((NT, 2, RANK, LANES), F32),
+            pltpu.VMEM((NT, 2, RANK, LANES), F32),
+            pltpu.VMEM((2, RANK, LANES), F32),
+            pltpu.VMEM((2 * NZ, RANK, LANES), F32),
+            pltpu.VMEM((RANK, LANES), F32),
             pltpu.VMEM((NZ, block, columns), F32),
             pltpu.VMEM((NZ, block, columns), F32),
             pltpu.VMEM((NZ, block, columns), F32),
             pltpu.VMEM((2, 8, block, columns), F32),
-            pltpu.VMEM((LANES, columns), F32),
-            pltpu.VMEM((2, RANK, LANES), F32),
-            pltpu.VMEM((2, NT, RANK, LANES), F32),
+            pltpu.VMEM((LANES, columns), jnp.bfloat16),
+            pltpu.VMEM((LANES, columns), jnp.bfloat16),
+            pltpu.VMEM((LANES, columns), jnp.bfloat16),
+            pltpu.VMEM((RANK, LANES), F32),
+            pltpu.VMEM((NT, RANK, LANES), F32),
             pltpu.VMEM((2, 2 * half, LANES), F32),
             pltpu.VMEM((2, half, LANES), F32),
             pltpu.VMEM((2, 4, half, LANES), F32),
@@ -361,18 +502,22 @@
             pltpu.VMEM((2, 2, half, LANES), F32),
             pltpu.VMEM((RANK, LANES), F32),
             pltpu.VMEM((2 * NZ, RANK, LANES), F32),
+            pltpu.VMEM((2 * NZ, LANES, 6 * RANK), jnp.bfloat16),
             dma((2, NZ)),
             dma((NZ,)), dma((NZ,)),
             dma((2, 8, CHUNKS)), dma((2, 8, CHUNKS)),
-            dma((2, NT)), dma((2, NT)),
+            dma((NT,)), dma((NT,)),
             dma((2,)), dma((2,)),
             dma((2, 4)), dma((2, 4)),
             dma((2, 4)), dma((2, 4)),
             dma((2,)), dma((2,)),
+            dma((NT,)), dma((NT,)),
+            dma((2,)), dma((2 * NZ,)),
+            dma((NT,)), dma, dma,
             dma, dma,
             dma((NT,)), dma((NT,)),
             dma((NZ,)), dma((NZ,)),
-            pltpu.SemaphoreType.REGULAR, pltpu.SemaphoreType.REGULAR,
+            pltpu.SemaphoreType.REGULAR, pltpu.SemaphoreType.REGULAR, pltpu.SemaphoreType.REGULAR((4,)),
         ],
         compiler_params=pltpu.CompilerParams(
             collective_id=0, has_side_effects=True, vmem_limit_bytes=52 * 2**20

time: 88.9 us -> 83.4 us (0.938)
  Pallas kernels: 85.6 us -> 80.1 us
    pallas_call x1, Pallas kernels: 85.6 us -> 80.1 us  [per_device(): pl.pallas_call(compress, out_shape=[jax.ShapeDtypeStruct(gradient.shape,...]
where the time goes in v3:
time: 83.4 us; the launch traced here: 83.2 us
  Pallas kernels  80.1 us (96%)
  local copies, waits for them, and re-layouts  2.46 us (3%)
    pallas_call x1, Pallas kernels, per_device(): pl.pallas_call(compress, out_shape=[jax.ShapeDtypeStruct(gradient.shape,...  80.1 us
    unnamed x4, local copies, waits for them, and re-layouts  2.46 us

profile of v3, /device:TPU:1, one launch (start us, length us, event | category | flops | bytes accessed | tf_op | source)
XLA Modules:
  0.0 83.2 jit_solution(15725945718385909844)
XLA Ops:
  0.6 0.0 copy-start
  0.6 0.7 copy-done
  1.3 80.1 %compress.1 = (bf16[1,3072,256]{2,1,0:T(8,128)(2,1)S(1)}, f32[16,256]{1,0:T(8,128)S(1)}) custom-call(bf16[1,3072,256]{2,1,0:T(8,128)(2,1)} %g_hbm.1, bf16[1,3072,256]{2,1,0:T(8,128)(2,1)} %e_hbm.1, f32[16,256]{1,0:T(8,128)S(1)} %copy-done), custom_call_target="tpu_custom_call" | custom-call | tf_op jit(solution)/shard_map/compress/pallas_call | solution.py:472
  81.4 1.1 %copy.7 = bf16[1,3072,256]{2,1,0:T(8,128)(2,1)} copy(bf16[1,3072,256]{2,1,0:T(8,128)(2,1)S(1)} %get-tuple-element.4) | data formatting | bytes 3145728
  82.6 0.6 copy.8
Async XLA Ops:
  0.6 0.7 copy-start

commit v4 on v3

--- a/solution.py
+++ b/solution.py
@@ -13,6 +13,7 @@
 LANES = 128
 NZ = 16
 NT = 16
+PIECES = 8
 CHUNKS = 4
 
 
@@ -45,8 +46,8 @@
 
 
 def compress(
-    g_hbm, e_hbm, q_hbm, out_ref, right_ref,
-    g_ref, e_ref, q_ref, early, early_in, early_sum, plane_in, first, own, cross, cross_in, ring, mean_top, mean_middle, mean_low, share, shares, term, pair, near, far, halves, relay, gathered, turned,
+    g_hbm, e_hbm, q_hbm, g_ref, e_ref, turned, stacked_ref, right_ref,
+    q_ref, early, early_in, early_sum, plane_in, first, own, cross, cross_in, ring, mean_top, mean_middle, mean_low, share, shares, term, pair, near, far, halves, relay, gathered,
     load_sem, cross_send, cross_recv, ring_send, ring_recv, share_send, share_recv,
     pair_send, pair_recv, near_send, near_recv, far_send, far_recv, half_send, half_recv,
     early_send, early_recv, plane_send, plane_recv, owner_send, owner_recv, q_sem,
@@ -449,17 +450,30 @@
     right_ref[...] = right
     weights = lax.dot_general(inverse, right, (((0,), (0,)), ((), ())), precision=HIGH, preferred_element_type=F32)
     top, middle, low = split_three(weights)
-    stacked = jnp.concatenate([top, top, middle, top, middle, low], axis=0)
-    for d in range(2 * NZ):
-        rows = pl.ds(d * block, block)
-        approx = jnp.dot(turned[d], stacked, preferred_element_type=F32)
-        total = g_ref[rows, :].astype(F32) + e_ref[rows, :].astype(F32)
-        out_ref[0, rows, :] = (total - approx[:block]).astype(jnp.bfloat16)
-
+    stacked_ref[...] = jnp.concatenate([top, top, middle, top, middle, low], axis=0)
     early_done()
     hand_done()
     for copy in sent:
         copy.wait_send()
+
+
+def residual(g_ref, e_ref, turned, stacked_ref, right_ref, out_hbm, right_hbm, out_ref, out_sem, right_sem):
+    blocks = turned.shape[0]
+    block = out_ref.shape[0] // blocks
+    copies = [pltpu.make_async_copy(right_ref, right_hbm, right_sem)]
+    copies[0].start()
+    each = blocks // PIECES
+    for piece in range(PIECES):
+        for d in range(piece * each, (piece + 1) * each):
+            rows = pl.ds(d * block, block)
+            approx = jnp.dot(turned[d], stacked_ref[...], preferred_element_type=F32)
+            total = g_ref[rows, :].astype(F32) + e_ref[rows, :].astype(F32)
+            out_ref[rows, :] = (total - approx[:block]).astype(jnp.bfloat16)
+        rows = pl.ds(piece * each * block, each * block)
+        copies.append(pltpu.make_async_copy(out_ref.at[rows], out_hbm.at[0, rows], out_sem.at[piece]))
+        copies[-1].start()
+    for copy in copies:
+        copy.wait()
 
 
 def per_device(gradient, error_in, q_start):
@@ -469,17 +483,18 @@
     vmem = pl.BlockSpec(memory_space=pltpu.VMEM)
     dma = pltpu.SemaphoreType.DMA
     half = RANK + 8
-    return pl.pallas_call(
+    kept = pl.pallas_call(
         compress,
         out_shape=[
-            jax.ShapeDtypeStruct(gradient.shape, gradient.dtype),
+            jax.ShapeDtypeStruct((rows, columns), jnp.bfloat16),
+            jax.ShapeDtypeStruct((rows, columns), jnp.bfloat16),
+            jax.ShapeDtypeStruct((2 * NZ, LANES, 6 * RANK), jnp.bfloat16),
+            jax.ShapeDtypeStruct((6 * RANK, columns), jnp.bfloat16),
             jax.ShapeDtypeStruct((RANK, columns), F32),
         ],
         in_specs=[hbm, hbm, hbm],
-        out_specs=[vmem, vmem],
+        out_specs=[vmem] * 5,
         scratch_shapes=[
-            pltpu.VMEM((rows, columns), jnp.bfloat16),
-            pltpu.VMEM((rows, columns), jnp.bfloat16),
             pltpu.VMEM((RANK, columns), F32),
             pltpu.VMEM((NT, 2, RANK, LANES), F32),
             pltpu.VMEM((NT, 2, RANK, LANES), F32),
@@ -502,7 +517,6 @@
             pltpu.VMEM((2, 2, half, LANES), F32),
             pltpu.VMEM((RANK, LANES), F32),
             pltpu.VMEM((2 * NZ, RANK, LANES), F32),
-            pltpu.VMEM((2 * NZ, LANES, 6 * RANK), jnp.bfloat16),
             dma((2, NZ)),
             dma((NZ,)), dma((NZ,)),
             dma((2, 8, CHUNKS)), dma((2, 8, CHUNKS)),
@@ -520,10 +534,22 @@
             pltpu.SemaphoreType.REGULAR, pltpu.SemaphoreType.REGULAR, pltpu.SemaphoreType.REGULAR((4,)),
         ],
         compiler_params=pltpu.CompilerParams(
-            collective_id=0, has_side_effects=True, vmem_limit_bytes=52 * 2**20
+            collective_id=0, has_side_effects=True, vmem_limit_bytes=49 * 2**20 + 2**18
         ),
         name="compress",
     )(gradient, error_in, q_start)
+    return pl.pallas_call(
+        residual,
+        out_shape=[
+            jax.ShapeDtypeStruct(gradient.shape, gradient.dtype),
+            jax.ShapeDtypeStruct((RANK, columns), F32),
+        ],
+        in_specs=[vmem] * 5,
+        out_specs=[hbm, hbm],
+        scratch_shapes=[pltpu.VMEM((rows, columns), jnp.bfloat16), dma((PIECES,)), dma],
+        compiler_params=pltpu.CompilerParams(vmem_limit_bytes=16 * 2**20),
+        name="residual",
+    )(*kept)
 
 
 def solution(mesh):

time: 83.4 us -> 82.4 us (0.988)
  local copies, waits for them, and re-layouts: 2.46 us -> 0.71 us
    unnamed x4 -> x2, local copies, waits for them, and re-layouts: 2.46 us -> 0.71 us
    pallas_call x1 -> x2, Pallas kernels: 80.1 us -> 80.9 us  [the longest x1 79.4 us: per_device(): pl.pallas_call(compress, out_shape=[jax.ShapeDtypeStruct((rows, columns),...]
where the time goes in v4:
time: 82.4 us; the launch traced here: 82.2 us
  Pallas kernels  80.9 us (98%)
    pallas_call x1, Pallas kernels, per_device(): pl.pallas_call(compress, out_shape=[jax.ShapeDtypeStruct((rows, columns),...  79.4 us

profile of v4, /device:TPU:1, one launch (start us, length us, event | category | flops | bytes accessed | tf_op | source)
XLA Modules:
  0.0 82.2 jit_solution(243983828749176318)
XLA Ops:
  0.6 0.0 copy-start
  0.6 0.7 copy-done
  1.3 79.4 %compress.1 = (bf16[3072,256]{1,0:T(8,128)(2,1)S(1)}, bf16[3072,256]{1,0:T(8,128)(2,1)S(1)}, bf16[32,128,96]{2,1,0:T(8,128)(2,1)S(1)}, bf16[96,256]{1,0:T(8,128)(2,1)S(1)}, f32[16,256]{1,0:T(8,128)S(1)}) custom-call(bf16[1,3072,256]{2,1,0:T(8,128)(2,1)} %g_hbm.1, bf16[1,3072,256]{2,1,0:T(8,128)(2,1)} %e_hbm.1, f32[16,256]{1,0:T(8,128)S(1)} %copy-done), custom_call_target="tpu_custom_call" | custom-call | tf_op jit(solution)/shard_map/compress/pallas_call | solution.py:486
  80.8 1.4 %residual.1 = (bf16[1,3072,256]{2,1,0:T(8,128)(2,1)}, f32[16,256]{1,0:T(8,128)}) custom-call(bf16[3072,256]{1,0:T(8,128)(2,1)S(1)} %get-tuple-element.7.g_ref, bf16[3072,256]{1,0:T(8,128)(2,1)S(1)} %get-tuple-element.8.e_ref, bf16[32,128,96]{2,1,0:T(8,128)(2,1)S(1)} %get-tuple-element.9.turned, bf16[96,256]{1,0:T(8,128)(2,1)S(1)} %get-tuple-element.10.stacked_ref, ...), custom_call_target="tpu_custom_call" | custom-call | tf_op jit(solution)/shard_map/residual/pallas_call | solution.py:541
Async XLA Ops:
  0.6 0.7 copy-start

commit v5 on v4

--- a/solution.py
+++ b/solution.py
@@ -436,7 +436,8 @@
         passing.append(
             send(gathered.at[source], gathered.at[source], pass_send.at[k], pass_recv.at[k], sibling)
         )
-        turn(source)
+    for k in range(1, NT):
+        turn(lax.rem(z - k + NZ, NZ) * 2 + core)
     for k, copy in enumerate(passing):
         copy.wait_recv()
         turn(lax.rem(z - k + NZ, NZ) * 2 + other)

time: 82.4 us -> 82.1 us (level)
  no operation moved by 1% of the time
where the time goes in v5:
time: 82.1 us; the launch traced here: 82 us
  Pallas kernels  80.6 us (98%)
    pallas_call x1, Pallas kernels, per_device(): pl.pallas_call(compress, out_shape=[jax.ShapeDtypeStruct((rows, columns),...  79.2 us

profile of v5, /device:TPU:1, one launch (start us, length us, event | category | flops | bytes accessed | tf_op | source)
XLA Modules:
  0.0 82.0 jit_solution(12519839393300388424)
XLA Ops:
  0.6 0.0 copy-start
  0.6 0.7 copy-done
  1.3 79.2 %compress.1 = (bf16[3072,256]{1,0:T(8,128)(2,1)S(1)}, bf16[3072,256]{1,0:T(8,128)(2,1)S(1)}, bf16[32,128,96]{2,1,0:T(8,128)(2,1)S(1)}, bf16[96,256]{1,0:T(8,128)(2,1)S(1)}, f32[16,256]{1,0:T(8,128)S(1)}) custom-call(bf16[1,3072,256]{2,1,0:T(8,128)(2,1)} %g_hbm.1, bf16[1,3072,256]{2,1,0:T(8,128)(2,1)} %e_hbm.1, f32[16,256]{1,0:T(8,128)S(1)} %copy-done), custom_call_target="tpu_custom_call" | custom-call | tf_op jit(solution)/shard_map/compress/pallas_call | solution.py:487
  80.5 1.4 %residual.1 = (bf16[1,3072,256]{2,1,0:T(8,128)(2,1)}, f32[16,256]{1,0:T(8,128)}) custom-call(bf16[3072,256]{1,0:T(8,128)(2,1)S(1)} %get-tuple-element.7.g_ref, bf16[3072,256]{1,0:T(8,128)(2,1)S(1)} %get-tuple-element.8.e_ref, bf16[32,128,96]{2,1,0:T(8,128)(2,1)S(1)} %get-tuple-element.9.turned, bf16[96,256]{1,0:T(8,128)(2,1)S(1)} %get-tuple-element.10.stacked_ref, ...), custom_call_target="tpu_custom_call" | custom-call | tf_op jit(solution)/shard_map/residual/pallas_call | solution.py:542
Async XLA Ops:
  0.6 0.7 copy-start
